TPU v7x, 32 devices: a whole 2x2x4 slice. The times are simulated.
32 devices in a mesh: groups: 2 (over y), seq: 4 (over z), heads: 2 (over x), section: 2 (over core).
Axes of the slice: x: 2, y: 2, z: 4, core: 2. Of those that a mesh axis runs over, the one named last changes fastest.
Arguments:
- prefill_q: bfloat16 [16384, 8192], P(('groups', 'seq', 'section'), 'heads'), parts along dimension 0, may hold values from -16 to 16
- prefill_kv: bfloat16 [16384, 2, 1024], P(('groups', 'seq', 'section'), None, 'heads'), parts along dimension 0, may hold values from -16 to 16
- lengths: int32 [4], P('groups'), parts along dimension 0, may hold values from 1024 to 4096, as said below
- decode_q: bfloat16 [128, 4, 8192], P(('groups', 'seq'), None, 'heads'), parts along dimension 0, may hold values from -16 to 16
- decode_kv: bfloat16 [128, 4, 2, 1024], P(('groups', 'seq'), None, None, 'heads'), parts along dimension 0, may hold values from -16 to 16
- row_cand: int32 [128], P(('groups', 'seq')), parts along dimension 0, may hold values from 0 to 1, as said below
- positions: int32 [128], P(('groups', 'seq')), parts along dimension 0, may hold values from 1 to 4096, as said below
- out_weight: bfloat16 [8192, 8192], P('heads', ('seq', 'section')), may hold values from -0.0625 to 0.0625
Outputs:
- prefill_out: bfloat16 [16384, 8192], P(('groups', 'seq', 'section'), 'heads'), parts along dimension 0
- decoded: bfloat16 [128, 4, 8192], P(('groups', 'heads'), None, ('seq', 'section')), parts along dimension 0
There are 2 independent parts, one for each index of `groups`. A program takes and returns all parts, laid end to end along the dimension named above; an argument that names none is the same for every part. Nothing has to cross between parts.
Inputs may be any that keep to these rules, and one draw needn't show every extreme that they name: `lengths`: each candidate's tokens sit at positions below its length; one candidate is full. `row_cand`: every candidate is continued by some row. `positions`: A row's count is at most the length of its candidate.
All inputs are finite; a program needn't handle non-finite values.
Results may differ from a plain program's by a relative error of at most 0.0065.
Values may be sent and summed in bfloat16 or wider, within the bound.
A program may use at most 384 MiB of HBM per device.

v0:
```python
import jax
import jax.numpy as jnp
from jax import lax
from jax.sharding import PartitionSpec as P

HD = 128
LEN = 4096


masked_score = -1e30


def shifted(array, axis, by):
    length = lax.axis_size(axis)
    pairs = [(i, i + by) for i in range(length) if 0 <= i + by < length]
    return lax.ppermute(array, axis, pairs)


def merged(value, axis, join):
    pieces = jax.tree.map(lambda part: lax.all_gather(part, axis), value)
    head = jax.tree.map(lambda part: part[0], pieces)
    tail = jax.tree.map(lambda part: part[1:], pieces)
    running, _ = lax.scan(lambda running, slab: (join(running, slab), None), head, tail)
    return running


def absorb(running, queries, key_rows, value_rows, visible, scaling):
    highest_old, total_old, summed_old = running
    scores = (
        jnp.einsum("qkgd,tkd->kgqt", queries, key_rows, preferred_element_type=jnp.float32)
        * scaling
    )
    scores = jnp.where(visible[None, None], scores, masked_score)
    highest_new = jnp.maximum(highest_old, jnp.max(scores, axis=-1))
    weights = jnp.where(visible[None, None], jnp.exp(scores - highest_new[..., None]), 0.0)
    rescale = jnp.exp(highest_old - highest_new)
    total_new = total_old * rescale + jnp.sum(weights, axis=-1)
    summed_new = summed_old * rescale[..., None] + jnp.einsum(
        "kgqt,tkd->kgqd",
        weights.astype(jnp.bfloat16),
        value_rows,
        preferred_element_type=jnp.float32,
    )
    return (highest_new, total_new, summed_new)


def join_parts(earlier, latter):
    highest = jnp.maximum(earlier[0], latter[0])
    scale_earlier = jnp.exp(earlier[0] - highest)
    scale_latter = jnp.exp(latter[0] - highest)
    totals = earlier[1] * scale_earlier + latter[1] * scale_latter
    summed = earlier[2] * scale_earlier[..., None] + latter[2] * scale_latter[..., None]
    return (highest, totals, summed)


def empty_state(kv_heads, group_size, query_count):
    return (
        jnp.full((kv_heads, group_size, query_count), masked_score, jnp.float32),
        jnp.zeros((kv_heads, group_size, query_count), jnp.float32),
        jnp.zeros((kv_heads, group_size, query_count, HD), jnp.float32),
    )


def body(prefill_q, prefill_kv, lengths, decode_q, decode_kv, row_cand, positions, out_weight):
    tok_local = prefill_q.shape[0]
    kv_heads = prefill_kv.shape[2] // HD
    group_size = prefill_q.shape[1] // HD // kv_heads
    scaling = HD ** (-0.5)
    shard_no = lax.axis_index(("seq", "section"))
    cand_ids = jnp.arange(lengths.shape[0])
    query_index = shard_no * tok_local + jnp.arange(tok_local)
    query_cand = query_index // LEN
    query_pos = query_index % LEN
    query_limit = jnp.sum(
        jnp.where(query_cand[:, None] == cand_ids[None, :], lengths[None, :], 0), axis=1
    )
    queries = prefill_q.reshape(tok_local, kv_heads, group_size, HD)

    def prefill_block(running, kv_block, first_index):
        key_index = first_index + jnp.arange(kv_block.shape[0])
        key_cand = key_index // LEN
        key_pos = key_index % LEN
        visible = (
            (key_cand[None, :] == query_cand[:, None])
            & (key_pos[None, :] <= query_pos[:, None])
            & (key_pos[None, :] < query_limit[:, None])
        )
        key_value = kv_block.reshape(kv_block.shape[0], 2, kv_heads, HD)
        return absorb(running, queries, key_value[:, 0], key_value[:, 1], visible, scaling)

    start_state = empty_state(kv_heads, group_size, tok_local)
    running = prefill_block(start_state, prefill_kv, shard_no * tok_local)

    def forward(turn_no, carried):
        kv_block, inner_state = carried
        kv_block = shifted(kv_block, ("seq", "section"), 1)
        return (
            kv_block,
            prefill_block(inner_state, kv_block, (shard_no - turn_no - 1) * tok_local),
        )

    running = lax.fori_loop(0, LEN // tok_local - 1, forward, (prefill_kv, running))[1]
    attended = running[2] / running[1][..., None]
    attended = jnp.where((query_pos < query_limit)[None, None, :, None], attended, 0.0)
    prefill_out = attended.transpose(2, 0, 1, 3).reshape(tok_local, -1).astype(jnp.bfloat16)
    row_count = decode_q.shape[0]
    step_count = decode_q.shape[1]
    query_rows = row_count * step_count
    all_queries, all_cands, all_limits = (
        lax.all_gather(decode_q, "seq", axis=0, tiled=True),
        lax.all_gather(row_cand, "seq", axis=0, tiled=True),
        lax.all_gather(positions, "seq", axis=0, tiled=True),
    )
    every_rows = all_queries.shape[0] * step_count
    local_index = shard_no * tok_local + jnp.arange(tok_local)
    key_value = prefill_kv.reshape(tok_local, 2, kv_heads, HD)
    visible = (local_index[None, :] // LEN == jnp.repeat(all_cands, step_count)[:, None]) & (
        local_index[None, :] % LEN < jnp.repeat(all_limits, step_count)[:, None]
    )
    every_queries = all_queries.reshape(every_rows, kv_heads, group_size, HD)
    local_scores = (
        jnp.einsum(
            "qkgd,tkd->kgqt", every_queries, key_value[:, 0], preferred_element_type=jnp.float32
        )
        * scaling
    )
    local_scores = jnp.where(visible[None, None], local_scores, masked_score)
    highest_all = lax.pmax(jnp.max(local_scores, axis=-1), "seq")
    local_weights = jnp.where(
        visible[None, None], jnp.exp(local_scores - highest_all[..., None]), 0.0
    )
    local_total = jnp.sum(local_weights, axis=-1)
    local_summed = jnp.einsum(
        "kgqt,tkd->kgqd",
        local_weights.astype(jnp.bfloat16),
        key_value[:, 1],
        preferred_element_type=jnp.float32,
    )
    total_mine, summed_mine = (
        lax.psum_scatter(local_total, "seq", scatter_dimension=2, tiled=True),
        lax.psum_scatter(local_summed, "seq", scatter_dimension=2, tiled=True),
    )
    highest_mine = lax.dynamic_slice_in_dim(
        highest_all, lax.axis_index("seq") * query_rows, query_rows, 2
    )
    running = (highest_mine, total_mine, summed_mine)
    running = merged(running, "section", join_parts)
    highest_old = running[0].reshape(kv_heads, group_size, row_count, step_count)
    total_old = running[1].reshape(kv_heads, group_size, row_count, step_count)
    summed_old = running[2].reshape(kv_heads, group_size, row_count, step_count, HD)
    new_pairs = decode_kv.reshape(row_count, step_count, 2, kv_heads, HD)
    query_five = decode_q.reshape(row_count, step_count, kv_heads, group_size, HD)
    new_scores = (
        jnp.einsum(
            "rskgd,rtkd->kgrst", query_five, new_pairs[:, :, 0], preferred_element_type=jnp.float32
        )
        * scaling
    )
    causal = jnp.arange(step_count)[None, :] <= jnp.arange(step_count)[:, None]
    new_scores = jnp.where(causal, new_scores, masked_score)
    highest_new = jnp.maximum(highest_old, jnp.max(new_scores, axis=-1))
    new_weights = jnp.where(causal, jnp.exp(new_scores - highest_new[..., None]), 0.0)
    rescale_old = jnp.exp(highest_old - highest_new)
    row_totals = total_old * rescale_old + jnp.sum(new_weights, axis=-1)
    summed_all = summed_old * rescale_old[..., None] + jnp.einsum(
        "kgrst,rtkd->kgrsd",
        new_weights.astype(jnp.bfloat16),
        new_pairs[:, :, 1],
        preferred_element_type=jnp.float32,
    )
    attention_rows = (
        (summed_all / row_totals[..., None])
        .transpose(2, 3, 0, 1, 4)
        .reshape(row_count, step_count, -1)
        .astype(jnp.bfloat16)
    )
    partial_terms = jnp.einsum(
        "rsc,cd->rsd",
        lax.all_gather(attention_rows, "seq", axis=0, tiled=True),
        out_weight,
        preferred_element_type=jnp.float32,
    )
    decoded = lax.psum_scatter(partial_terms, "heads", scatter_dimension=0, tiled=True).astype(
        jnp.bfloat16
    )
    return (prefill_out, decoded)


def solution(mesh):
    return jax.shard_map(
        body,
        mesh=mesh,
        in_specs=(
            P(("groups", "seq", "section"), "heads"),
            P(("groups", "seq", "section"), None, "heads"),
            P("groups"),
            P(("groups", "seq"), None, "heads"),
            P(("groups", "seq"), None, None, "heads"),
            P(("groups", "seq")),
            P(("groups", "seq")),
            P("heads", ("seq", "section")),
        ),
        out_specs=(
            P(("groups", "seq", "section"), "heads"),
            P(("groups", "heads"), None, ("seq", "section")),
        ),
        check_vma=False,
    )
```

profile of v0, /device:TPU:9, one launch (start us, length us, event | category | flops | bytes accessed | tf_op | source)
XLA Modules:
  0.0 909.8 jit_solution(6347154467377810478)
XLA Ops:
  11.6 6.4 all-reduce.2
  18.4 6.2 copy.106
  26.2 28.6 %all-gather.7.cloned.1.call-done = bf16[64,4,4096]{2,1,0:T(4,128)(2,1)} async-done(((bf16[16,4,4096]{2,1,0:T(4,128)(2,1)}), bf16[64,4,4096]{2,1,0:T(4,128)(2,1)}) %all-gather.7.cloned.1.call-update) | async-done | bytes 2097168 | tf_op jit(solution)/shard_map/all_gather | solution.py:110
  58.6 15.5 %fusion.32 = (f32[4,8,256]{2,1,0:T(8,128)S(1)}, f32[4,1024,256,8]{2,1,3,0:T(8,128)}) fusion(pred[256,1024]{0,1:T(8,128)(4,1)S(1)} %compare_and_fusion.2, bf16[256,4,8,128]{3,2,1,0:T(8,128)(2,1)S(1)} %reshape.511, bf16[1024,2,4,128]{0,3,2,1:T(8,128)(2,1)} %bitcast), kind=kOutput, calls=%fused_computation.52 | convolution fusion | flops 2172641280 | bytes 36995072 | tf_op jit(solution)/shard_map/qkgd,tkd->kgqt/dot_general | solution.py:122
  74.1 12.6 %pmax.7 = f32[4,8,256]{2,1,0:T(8,128)S(1)} all-reduce(f32[4,8,256]{2,1,0:T(8,128)S(1)} %get-tuple-element.443), channel_id=1, replica_groups=mesh['groups'=2,'seq'=4,'heads'=2,'section'=2] {'seq'}, use_global_device_ids=true, to_apply=%region_8.9 | all-reduce | flops 8192 | bytes 65536 | tf_op jit(solution)/shard_map/pmax | solution.py:128
  86.7 17.6 %fusion.35 = f32[4,8,256,128]{3,2,1,0:T(8,128)} fusion(f32[4,1024,256,8]{2,1,3,0:T(8,128)} %get-tuple-element.444, f32[4,8,256]{2,1,0:T(8,128)S(1)} %pmax.7, pred[256,1024]{0,1:T(8,128)(4,1)S(1)} %compare_and_fusion.2, bf16[1024,2,4,128]{0,3,2,1:T(8,128)(2,1)} %bitcast), kind=kOutput, calls=%fused_computation.56 | convolution fusion | flops 2189426688 | bytes 39092224 | tf_op jit(solution)/shard_map/kgqt,tkd->kgqd/dot_general | solution.py:133
  108.4 11.7 %copy.102 = bf16[1024,4096]{0,1:T(8,128)(2,1)} copy(bf16[1024,4096]{1,0:T(8,128)(2,1)} %param.10) | data formatting | bytes 16777216 | tf_op args[0]
  120.1 48.2 %fusion.26 = (f32[4,8,1024]{2,1,0:T(8,128)S(1)}, f32[4,1024,1024,8]{2,1,3,0:T(8,128)}) fusion(pred[1024,1024]{0,1:T(8,128)(4,1)S(1)} %compare_and_fusion.1, bf16[1024,4,8,128]{0,3,2,1:T(8,128)(2,1)} %bitcast.183, bf16[1024,2,4,128]{0,3,2,1:T(8,128)(2,1)} %bitcast), kind=kOutput, calls=%fused_computation.45 | convolution fusion | flops 8690565120 | bytes 144834560 | tf_op jit(solution)/shard_map/qkgd,tkd->kgqt/dot_general | solution.py:30
  168.3 15.1 %fusion.33 = f32[4,8,256]{2,1,0:T(8,128)S(1)} fusion(f32[4,1024,256,8]{2,1,3,0:T(8,128)} %get-tuple-element.444, f32[4,8,256]{2,1,0:T(8,128)S(1)} %pmax.7, pred[256,1024]{0,1:T(8,128)(4,1)S(1)} %compare_and_fusion.2), kind=kLoop, calls=%fused_computation.53 | loop fusion | flops 41934848 | bytes 33882112 | tf_op jit(solution)/shard_map/reduce_sum | solution.py:132
  185.8 42.6 %fusion.28 = f32[4,8,1024]{2,1,0:T(8,128)S(1)} fusion(f32[4,1024,1024,8]{2,1,3,0:T(8,128)} %get-tuple-element.442, f32[4,8,1024]{2,1,0:T(8,128)} %broadcast_maximum_fusion, pred[1024,1024]{0,1:T(8,128)(4,1)S(1)} %compare_and_fusion.1), kind=kLoop, calls=%fused_computation.47 | loop fusion | flops 167739392 | bytes 135528448 | tf_op jit(solution)/shard_map/reduce_sum | solution.py:37
  233.0 5.4 all-gather.1
  250.3 56.1 %fusion.38 = f32[4,8,1024,128]{3,2,1,0:T(8,128)} fusion(f32[4,1024,1024,8]{2,1,3,0:T(8,128)} %get-tuple-element.442, f32[4,8,1024]{2,1,0:T(8,128)} %broadcast_maximum_fusion, pred[1024,1024]{0,1:T(8,128)(4,1)S(1)} %compare_and_fusion.1, f32[4,8,1024]{2,1,0:T(8,128)} %get-tuple-element.435, bf16[1024,2,4,128]{0,3,2,1:T(8,128)(2,1)} %bitcast), kind=kOutput, calls=%fused_computation.58 | convolution fusion | flops 8761901056 | bytes 153354240 | tf_op jit(solution)/shard_map/kgqt,tkd->kgqd/dot_general | solution.py:38
  306.4 11.3 %copy.107 = bf16[1024,4,8,128]{3,0,2,1:T(8,128)(2,1)} copy(bf16[1024,4,8,128]{0,3,2,1:T(8,128)(2,1)} %bitcast.184) | data formatting | bytes 16777216
  319.0 7.3 fusion.41
  326.3 536.0 %while.30 = (s32[]{:T(128)}, bf16[1024,2,512]{0,2,1:T(8,128)(2,1)}, f32[4,8,1024]{2,1,0:T(8,128)}, f32[4,8,1024]{2,1,0:T(8,128)S(1)}, f32[4,8,1024,128]{3,2,1,0:...) while((s32[]{:T(128)}, bf16[1024,2,512]{0,2,1:T(8,128)(2,1)}, ...), condition=%wide.region_6.7_spmd.clone.clone, body=%wide.region_3.6_spmd.clone.clone.sunk | while | flops 17629814784 | bytes 465604800 | solution.py:102
  333.8 19.4 %collective-permute-done = bf16[1024,2,512]{0,2,1:T(8,128)(2,1)S(1)} collective-permute-done((bf16[1024,2,512]{0,2,1:T(8,128)(2,1)}, bf16[1024,2,512]{0,2,1:T(8,128)(2,1)S(1)}, u32[]{:S(2)}, u32[]{:S(2)}) %collective-permute-start) | collective-permute-done | bytes 2097184 | tf_op jit(solution)/shard_map/while/body/eval_jaxpr/ppermute | solution.py:16
  353.2 47.6 %fusion.96 = (f32[4,8,1024]{2,1,0:T(8,128)S(1)}, f32[4,1024,1024,8]{2,1,3,0:T(8,128)}) fusion(pred[1024,1024]{0,1:T(8,128)(4,1)S(1)} %compare_and_fusion.4, bf16[1024,4,8,128]{3,0,2,1:T(8,128)(2,1)} %get-tuple-element.557, bf16[1024,2,4,128]{0,3,2,1:T(8,128)(2,1)S(1)} %bitcast.181), kind=kOutput, calls=%fused_computation.4.clone.2 | convolution fusion | flops 8690565120 | bytes 144834560 | tf_op jit(solution)/shard_map/while/body/eval_jaxpr/qkgd,tkd->kgqt/dot_general | solution.py:30
  401.7 41.3 %fusion.97 = f32[4,8,1024]{2,1,0:T(8,128)S(1)} fusion(f32[4,1024,1024,8]{2,1,3,0:T(8,128)} %get-tuple-element.523, f32[4,8,1024]{2,1,0:T(8,128)S(1)} %max.57, pred[1024,1024]{0,1:T(8,128)(4,1)S(1)} %compare_and_fusion.4), kind=kLoop, calls=%fused_computation.6.clone.1 | loop fusion | flops 167739392 | bytes 135528448 | tf_op jit(solution)/shard_map/while/body/eval_jaxpr/reduce_sum | solution.py:37
  444.6 58.6 %multiply_add_fusion.6 = f32[4,8,1024,128]{3,2,1,0:T(8,128)} fusion(f32[4,8,1024,128]{3,2,1,0:T(8,128)} %get-tuple-element.542, f32[4,1024,1024,8]{2,1,3,0:T(8,128)} %get-tuple-element.523, f32[4,8,1024]{2,1,0:T(8,128)S(1)} %max.57, pred[1024,1024]{0,1:T(8,128)(4,1)S(1)} %compare_and_fusion.4, f32[4,8,1024]{2,1,0:T(8,128)S(1)} %get-tuple-element.525, ...), kind=kOutput, calls=%fused_computation.9.clone.3 | convolution fusion | flops 8766095360 | bytes 170131456 | tf_op jit(solution)/shard_map/while/body/eval_jaxpr/kgqt,tkd->kgqd/dot_general | solution.py:38
  504.5 4.3 collective-permute-start
  512.7 19.4 %collective-permute-done = bf16[1024,2,512]{0,2,1:T(8,128)(2,1)S(1)} collective-permute-done((bf16[1024,2,512]{0,2,1:T(8,128)(2,1)}, bf16[1024,2,512]{0,2,1:T(8,128)(2,1)S(1)}, u32[]{:S(2)}, u32[]{:S(2)}) %collective-permute-start) | collective-permute-done | bytes 2097184 | tf_op jit(solution)/shard_map/while/body/eval_jaxpr/ppermute | solution.py:16
  532.1 47.6 %fusion.96 = (f32[4,8,1024]{2,1,0:T(8,128)S(1)}, f32[4,1024,1024,8]{2,1,3,0:T(8,128)}) fusion(pred[1024,1024]{0,1:T(8,128)(4,1)S(1)} %compare_and_fusion.4, bf16[1024,4,8,128]{3,0,2,1:T(8,128)(2,1)} %get-tuple-element.557, bf16[1024,2,4,128]{0,3,2,1:T(8,128)(2,1)S(1)} %bitcast.181), kind=kOutput, calls=%fused_computation.4.clone.2 | convolution fusion | flops 8690565120 | bytes 144834560 | tf_op jit(solution)/shard_map/while/body/eval_jaxpr/qkgd,tkd->kgqt/dot_general | solution.py:30
  580.6 41.3 %fusion.97 = f32[4,8,1024]{2,1,0:T(8,128)S(1)} fusion(f32[4,1024,1024,8]{2,1,3,0:T(8,128)} %get-tuple-element.523, f32[4,8,1024]{2,1,0:T(8,128)S(1)} %max.57, pred[1024,1024]{0,1:T(8,128)(4,1)S(1)} %compare_and_fusion.4), kind=kLoop, calls=%fused_computation.6.clone.1 | loop fusion | flops 167739392 | bytes 135528448 | tf_op jit(solution)/shard_map/while/body/eval_jaxpr/reduce_sum | solution.py:37
  623.5 58.6 %multiply_add_fusion.6 = f32[4,8,1024,128]{3,2,1,0:T(8,128)} fusion(f32[4,8,1024,128]{3,2,1,0:T(8,128)} %get-tuple-element.542, f32[4,1024,1024,8]{2,1,3,0:T(8,128)} %get-tuple-element.523, f32[4,8,1024]{2,1,0:T(8,128)S(1)} %max.57, pred[1024,1024]{0,1:T(8,128)(4,1)S(1)} %compare_and_fusion.4, f32[4,8,1024]{2,1,0:T(8,128)S(1)} %get-tuple-element.525, ...), kind=kOutput, calls=%fused_computation.9.clone.3 | convolution fusion | flops 8766095360 | bytes 170131456 | tf_op jit(solution)/shard_map/while/body/eval_jaxpr/kgqt,tkd->kgqd/dot_general | solution.py:38
  683.4 4.3 collective-permute-start
  691.6 19.4 %collective-permute-done = bf16[1024,2,512]{0,2,1:T(8,128)(2,1)S(1)} collective-permute-done((bf16[1024,2,512]{0,2,1:T(8,128)(2,1)}, bf16[1024,2,512]{0,2,1:T(8,128)(2,1)S(1)}, u32[]{:S(2)}, u32[]{:S(2)}) %collective-permute-start) | collective-permute-done | bytes 2097184 | tf_op jit(solution)/shard_map/while/body/eval_jaxpr/ppermute | solution.py:16
  711.0 47.6 %fusion.96 = (f32[4,8,1024]{2,1,0:T(8,128)S(1)}, f32[4,1024,1024,8]{2,1,3,0:T(8,128)}) fusion(pred[1024,1024]{0,1:T(8,128)(4,1)S(1)} %compare_and_fusion.4, bf16[1024,4,8,128]{3,0,2,1:T(8,128)(2,1)} %get-tuple-element.557, bf16[1024,2,4,128]{0,3,2,1:T(8,128)(2,1)S(1)} %bitcast.181), kind=kOutput, calls=%fused_computation.4.clone.2 | convolution fusion | flops 8690565120 | bytes 144834560 | tf_op jit(solution)/shard_map/while/body/eval_jaxpr/qkgd,tkd->kgqt/dot_general | solution.py:30
  759.5 41.3 %fusion.97 = f32[4,8,1024]{2,1,0:T(8,128)S(1)} fusion(f32[4,1024,1024,8]{2,1,3,0:T(8,128)} %get-tuple-element.523, f32[4,8,1024]{2,1,0:T(8,128)S(1)} %max.57, pred[1024,1024]{0,1:T(8,128)(4,1)S(1)} %compare_and_fusion.4), kind=kLoop, calls=%fused_computation.6.clone.1 | loop fusion | flops 167739392 | bytes 135528448 | tf_op jit(solution)/shard_map/while/body/eval_jaxpr/reduce_sum | solution.py:37
  802.4 58.6 %multiply_add_fusion.6 = f32[4,8,1024,128]{3,2,1,0:T(8,128)} fusion(f32[4,8,1024,128]{3,2,1,0:T(8,128)} %get-tuple-element.542, f32[4,1024,1024,8]{2,1,3,0:T(8,128)} %get-tuple-element.523, f32[4,8,1024]{2,1,0:T(8,128)S(1)} %max.57, pred[1024,1024]{0,1:T(8,128)(4,1)S(1)} %compare_and_fusion.4, f32[4,8,1024]{2,1,0:T(8,128)S(1)} %get-tuple-element.525, ...), kind=kOutput, calls=%fused_computation.9.clone.3 | convolution fusion | flops 8766095360 | bytes 170131456 | tf_op jit(solution)/shard_map/while/body/eval_jaxpr/kgqt,tkd->kgqd/dot_general | solution.py:38
  862.3 10.7 %fusion.43 = bf16[1024,4,8,128]{3,0,2,1:T(8,128)(2,1)} fusion(f32[4,8,1024,128]{3,2,1,0:T(8,128)} %get-tuple-element.301, f32[4,8,1024]{2,1,0:T(8,128)S(1)} %get-tuple-element.302, pred[1024]{0:T(1024)(128)(4,1)S(1)} %copy-done.3), kind=kLoop, calls=%fused_computation.62 | loop fusion | flops 12582912 | bytes 25297920 | tf_op jit(solution)/shard_map/convert_element_type | solution.py:105
  873.0 12.0 %copy.108 = bf16[1024,4,8,128]{3,2,1,0:T(8,128)(2,1)} copy(bf16[1024,4,8,128]{3,0,2,1:T(8,128)(2,1)} %fusion.43) | data formatting | bytes 16777216 | tf_op jit(solution)/shard_map/convert_element_type | solution.py:105
  885.0 15.5 %copy.160 = bf16[128,8,32,128]{3,1,2,0:T(8,128)(2,1)} copy(bf16[128,8,32,128]{3,2,1,0:T(8,128)(2,1)} %bitcast.185) | data formatting | bytes 16777216
  (92 shorter events, 62.0 us)
Async XLA Ops:
  7.2 47.7 %all-gather.7.cloned.1.call-start = ((), (), s32[]{:S(2)}) async-start(), calls=%async_computation.3 | async-start | bytes 2621440 | tf_op jit(solution)/shard_map/all_gather | solution.py:110
  7.9 177.9 %reduce-scatter.6.cloned.1.call-start = ((), (), s32[]{:S(2)}) async-start(), calls=%async_computation.4 | async-start | bytes 5242880 | tf_op jit(solution)/shard_map/reduce_scatter | solution.py:141
  104.4 134.8 %reduce-scatter.10.cloned.1.call-start = ((), (), s32[]{:S(2)}) async-start(), calls=%async_computation.8 | async-start | bytes 163840
  184.6 58.8 %all-gather.11.cloned.1.call-start = ((), (), s32[]{:S(2)}) async-start(), calls=%async_computation.7 | async-start | bytes 3145728 | tf_op jit(solution)/shard_map/all_gather | solution.py:20
  185.8 133.2 %all-gather.9.cloned.1.call-start = ((), (), s32[]{:S(2)}) async-start(), calls=%async_computation.5 | async-start | bytes 2621440 | tf_op jit(solution)/shard_map/all_gather | solution.py:179
  185.8 42.6 %copy-start = (bf16[16,4,4096]{2,1,0:T(4,128)(2,1)S(1)}, bf16[16,4,4096]{2,1,0:T(4,128)(2,1)}, u32[]{:S(2)}) copy-start(bf16[16,4,4096]{2,1,0:T(4,128)(2,1)} %param.13) | copy-start | bytes 1572868
  185.8 43.1 %copy-start.2 = (bf16[16,4,2,512]{3,2,1,0:T(2,128)(2,1)S(1)}, bf16[16,4,2,512]{3,2,1,0:T(2,128)(2,1)}, u32[]{:S(2)}) copy-start(bf16[16,4,2,512]{3,2,1,0:T(2,128)(2,1)} %param.14) | copy-start | bytes 393220
  232.9 10.5 %copy-start.1 = (f32[4,8,16,4,4]{1,4,3,2,0:T(4,128)}, f32[4,8,16,4,4]{1,4,3,2,0:T(4,128)S(1)}, u32[]{:S(2)}) copy-start(f32[4,8,16,4,4]{1,4,3,2,0:T(4,128)S(1)} %get-tuple-element.446) | copy-start | bytes 98308
  250.2 650.3 %reduce-scatter.8.cloned.1.call-start = ((), (), s32[]{:S(2)}) async-start(), calls=%async_computation.6 | async-start | bytes 1572864 | tf_op jit(solution)/shard_map/reduce_scatter | solution.py:183
  326.3 536.0 %copy-start.3 = (pred[1024]{0:T(1024)(128)(4,1)S(1)}, pred[1024]{0:T(1024)(128)(4,1)}, u32[]{:S(2)}) copy-start(pred[1024]{0:T(1024)(128)(4,1)} %fusion.66) | copy-start | bytes 3076
  326.5 26.7 %collective-permute-start = (bf16[1024,2,512]{0,2,1:T(8,128)(2,1)}, bf16[1024,2,512]{0,2,1:T(8,128)(2,1)S(1)}, u32[]{:S(2)}, u32[]{:S(2)}) collective-permute-start(bf16[1024,2,512]{0,2,1:T(8,128)(2,1)} %get-tuple-element.539), channel_id=1, source_target_pairs={{0,1},{1,4},{4,5},{5,8},{8,9},{9,12},{12,13},{2,3},{3,6},{6,7},{7,... | collective-permute-start | bytes 6291464 | tf_op jit(solution)/shard_map/while/body/eval_jaxpr/ppermute | solution.py:16
  504.5 27.5 %collective-permute-start = (bf16[1024,2,512]{0,2,1:T(8,128)(2,1)}, bf16[1024,2,512]{0,2,1:T(8,128)(2,1)S(1)}, u32[]{:S(2)}, u32[]{:S(2)}) collective-permute-start(bf16[1024,2,512]{0,2,1:T(8,128)(2,1)} %get-tuple-element.539), channel_id=1, source_target_pairs={{0,1},{1,4},{4,5},{5,8},{8,9},{9,12},{12,13},{2,3},{3,6},{6,7},{7,... | collective-permute-start | bytes 6291464 | tf_op jit(solution)/shard_map/while/body/eval_jaxpr/ppermute | solution.py:16
  683.4 27.5 %collective-permute-start = (bf16[1024,2,512]{0,2,1:T(8,128)(2,1)}, bf16[1024,2,512]{0,2,1:T(8,128)(2,1)S(1)}, u32[]{:S(2)}, u32[]{:S(2)}) collective-permute-start(bf16[1024,2,512]{0,2,1:T(8,128)(2,1)} %get-tuple-element.539), channel_id=1, source_target_pairs={{0,1},{1,4},{4,5},{5,8},{8,9},{9,12},{12,13},{2,3},{3,6},{6,7},{7,... | collective-permute-start | bytes 6291464 | tf_op jit(solution)/shard_map/while/body/eval_jaxpr/ppermute | solution.py:16
Sparse Core Ops, SparseCore 0:
  9.6 45.2 all-gather.6
  104.5 81.2 reduce-scatter.5
  188.1 15.9 reduce-scatter.9
  205.5 14.0 all-gather.10
  250.3 44.7 all-gather.8
  326.4 21.0 reduce-scatter.7
where the time goes:
time: 922 us; the launch traced here: 910 us
  matrix products  469 us (51%)
  other arithmetic  220 us (24%)
  waiting for transfers between devices  88.1 us (10%)
  local copies, waits for them, and re-layouts  78.5 us (9%)
  blocking collectives  26.6 us (3%)
  between operations  15.5 us (2%)
  starting transfers between devices  12.4 us (1%)
    dot_general x4, matrix products, absorb(): jnp.einsum('kgqt,tkd->kgqd', weights.astype(jnp.bfloat16), value_rows, pr...  232 us
    dot_general x4, matrix products, absorb(): jnp.einsum('qkgd,tkd->kgqt', queries, key_rows, preferred_element_type=jn...  191 us
    reduce_sum x4, other arithmetic, absorb(): total_new = total_old * rescale + jnp.sum(weights, axis=-1)  166 us
    ppermute x3, waiting for transfers between devices, shifted(): return lax.ppermute(array, axis, pairs)  58.3 us
    unnamed x22, local copies, waits for them, and re-layouts  50.7 us
    all_gather x1, waiting for transfers between devices, body(): lax.all_gather(decode_q, 'seq', axis=0, tiled=True)  28.6 us
  transfers between devices with their start and end apart: 9, of which 5 were waited for; matrix products, arithmetic and copies ran while one was open for 78% of the time, Pallas kernels for 0%

commit v1 on v0

v1 whole, which is shorter than its diff:
```python
import functools
import math

import jax
import jax.numpy as jnp
from jax import lax
from jax.experimental import pallas as pl
from jax.experimental.pallas import tpu as pltpu
from jax.sharding import PartitionSpec as P

HD = 128
LEN = 4096
TQ = 256
masked_score = -1e30
SCALE2 = math.log2(math.e) * HD ** (-0.5)


def scores_of(queries, keys):
    return lax.dot_general(
        queries, keys, (((1,), (1,)), ((), ())), preferred_element_type=jnp.float32
    )


def with_ones(values):
    return jnp.concatenate([values, jnp.ones_like(values)], axis=1)


def absorb(highest_ref, sums_ref, rows, scores, values):
    old = highest_ref[rows, :1]
    new = jnp.maximum(old, jnp.max(scores, axis=1, keepdims=True))
    weights = jnp.exp2((scores - new) * SCALE2).astype(jnp.bfloat16)
    rescale = jnp.exp2((old - new) * SCALE2)
    sums_ref[rows, :] = sums_ref[rows, :] * rescale + jnp.dot(
        weights, with_ones(values), preferred_element_type=jnp.float32
    )
    highest_ref[rows, :] = jnp.broadcast_to(new, (new.shape[0], HD))


def start(highest_ref, sums_ref):
    highest_ref[...] = jnp.full(highest_ref.shape, masked_score, jnp.float32)
    sums_ref[...] = jnp.zeros(sums_ref.shape, jnp.float32)


def near_kernel(place, q, k_own, v_own, k_mate, v_mate, out, lse, highest, sums):
    tokens = q.shape[0]
    tile = min(TQ, tokens)
    start(highest, sums)

    @pl.when(place[0] == 1)
    def _():
        for at in range(0, tokens, tile):
            absorb(
                highest, sums, pl.ds(at, tile), scores_of(q[pl.ds(at, tile), :], k_mate[...]), v_mate[...]
            )

    for at in range(0, tokens, tile):
        rows = pl.ds(at, tile)
        scores = scores_of(q[rows, :], k_own[: at + tile, :])
        shape = scores.shape
        seen = lax.broadcasted_iota(jnp.int32, shape, 1) <= at + lax.broadcasted_iota(
            jnp.int32, shape, 0
        )
        absorb(highest, sums, rows, jnp.where(seen, scores, masked_score), v_own[: at + tile, :])
        total = sums[rows, HD:]
        out[rows, :] = sums[rows, :HD] / total
        lse[rows, :] = highest[rows, :] + jnp.log2(total) * (1.0 / SCALE2)


def far_kernel(place, q, k_one, v_one, k_two, v_two, near, lse, out, highest, sums):
    tokens = q.shape[0]
    tile = min(TQ, tokens)
    chips, limit = place[1], place[2]
    highest[...] = lse[...]
    sums[:, :HD] = near[...]
    sums[:, HD:] = jnp.ones((tokens, HD), jnp.float32)

    @pl.loop(0, chips)
    def _(chip):
        keys = pl.ds(pl.multiple_of(chip * tokens, tokens), tokens)
        for k, v in ((k_one, v_one), (k_two, v_two)):
            for at in range(0, tokens, tile):
                rows = pl.ds(at, tile)
                absorb(highest, sums, rows, scores_of(q[rows, :], k[keys, :]), v[keys, :])

    position = place[3] + lax.broadcasted_iota(jnp.int32, (tokens, HD), 0)
    attended = sums[:, :HD] / sums[:, HD:]
    out[...] = jnp.where(position < limit, attended, 0.0).astype(out.dtype)


def decode_kernel(
    group, steps, place, q, k_new, v_new, k_own, v_own, k_mate, v_mate,
    k_one, v_one, k_two, v_two, limits, out, highest, sums,
):
    tokens = k_own.shape[0]
    count = q.shape[0]
    queries = jnp.concatenate([q[:, h * HD : (h + 1) * HD] for h in range(group)], axis=0)
    start(highest, sums)
    every = pl.ds(0, group * count)
    shape = (group * count, count)
    asked = lax.rem(lax.broadcasted_iota(jnp.int32, shape, 0), count)
    key = lax.broadcasted_iota(jnp.int32, shape, 1)
    seen = (lax.div(asked, steps) == lax.div(key, steps)) & (key <= asked)
    absorb(
        highest, sums, every,
        jnp.where(seen, scores_of(queries, k_new[...]), masked_score), v_new[...],
    )
    limit = jnp.concatenate([limits[:, :1]] * group, axis=0)

    def block(k, v, keys, base):
        scores = scores_of(queries, k[keys, :])
        position = base + lax.broadcasted_iota(jnp.int32, scores.shape, 1)
        absorb(
            highest, sums, every, jnp.where(position < limit, scores, masked_score), v[keys, :]
        )

    block(k_own, v_own, pl.ds(0, tokens), place[0])
    block(k_mate, v_mate, pl.ds(0, tokens), place[1])

    @pl.loop(0, k_one.shape[0] // tokens)
    def _(chip):
        keys = pl.ds(pl.multiple_of(chip * tokens, tokens), tokens)
        block(k_one, v_one, keys, place[2 + 2 * chip])
        block(k_two, v_two, keys, place[3 + 2 * chip])

    for h in range(group):
        rows = pl.ds(h * count, count)
        out[:, h * HD : (h + 1) * HD] = (sums[rows, :HD] / sums[rows, HD:]).astype(out.dtype)


def column(rows, at, width=HD):
    return pl.BlockSpec((rows, width), lambda h, place: (0, at(h)))


def body(mesh_shape, prefill_q, prefill_kv, lengths, decode_q, decode_kv, row_cand, positions, out_weight):
    tokens = prefill_q.shape[0]
    heads = prefill_q.shape[1] // HD
    width = prefill_kv.shape[2]
    kv_heads = width // HD
    group = heads // kv_heads
    seqs, sections = mesh_shape["seq"], mesh_shape["section"]
    chips = LEN // (tokens * sections)
    shards = chips * sections
    z, section = lax.axis_index("seq"), lax.axis_index("section")
    cand, chip = z // chips, z % chips
    row_count, steps = decode_q.shape[:2]
    count = row_count * steps

    kv = prefill_kv.reshape(tokens, 2 * width)
    swap = [(i, sections - 1 - i) for i in range(sections)]
    mate = lax.ppermute(kv, "section", swap)
    ones = [
        lax.ppermute(
            kv, "seq", [(i, i // chips * chips + (i % chips + d) % chips) for i in range(seqs)]
        )
        for d in range(1, chips)
    ]
    spread = [
        (j * sections + c, c * shards + j) for j in range(seqs) for c in range(sections)
    ]
    new = jnp.concatenate(
        [decode_q.reshape(count, -1), decode_kv.reshape(count, -1)], axis=1
    )
    new = lax.ppermute(new, ("seq", "section"), spread)
    all_cands = lax.all_gather(row_cand, "seq", axis=0, tiled=True)
    all_limits = lax.all_gather(positions, "seq", axis=0, tiled=True)
    limit = jnp.sum(jnp.where(jnp.arange(lengths.shape[0]) == cand, lengths, 0))
    start_at = (chip * sections + section) * tokens
    place = jnp.stack([section, chip, limit, start_at]).astype(jnp.int32)

    block_ops = tokens * tokens * HD * heads * 4
    params = pltpu.CompilerParams(
        dimension_semantics=("arbitrary",), vmem_limit_bytes=56 * 2**20
    )
    of_query = column(tokens, lambda h: h)
    of_key = column(tokens, lambda h: h // group)
    of_value = column(tokens, lambda h: kv_heads + h // group)
    state = [pltpu.VMEM((tokens, HD), jnp.float32), pltpu.VMEM((tokens, 2 * HD), jnp.float32)]
    near, lse = pl.pallas_call(
        near_kernel,
        out_shape=[jax.ShapeDtypeStruct((tokens, heads * HD), jnp.float32)] * 2,
        grid_spec=pltpu.PrefetchScalarGridSpec(
            num_scalar_prefetch=1,
            grid=(heads,),
            in_specs=[of_query, of_key, of_value, of_key, of_value],
            out_specs=[of_query, of_query],
            scratch_shapes=state,
        ),
        compiler_params=params,
        cost_estimate=pl.CostEstimate(
            flops=3 * block_ops, bytes_accessed=2**26, transcendentals=0
        ),
        name="near",
    )(place, prefill_q, kv, kv, mate, mate)

    one = jnp.concatenate(ones, axis=0) if len(ones) > 1 else ones[0]
    two = lax.ppermute(one, "section", swap)

    slot = chip * sections + section
    my_cands = lax.dynamic_slice_in_dim(all_cands, slot * row_count, row_count)
    my_limits = lax.dynamic_slice_in_dim(all_limits, slot * row_count, row_count)
    my_limits = jnp.repeat(jnp.where(my_cands == cand, my_limits, 0), steps)
    bases = [start_at, (chip * sections + 1 - section) * tokens]
    for d in range(1, chips):
        other = (chip - d) % chips
        bases += [(other * sections + section) * tokens, (other * sections + 1 - section) * tokens]
    far_rows = one.shape[0]
    key_at, value_at = (lambda h: h), (lambda h: kv_heads + h)
    new_at = heads
    decode_out = pl.pallas_call(
        functools.partial(decode_kernel, group, steps),
        out_shape=jax.ShapeDtypeStruct((count, heads * HD), jnp.bfloat16),
        grid_spec=pltpu.PrefetchScalarGridSpec(
            num_scalar_prefetch=1,
            grid=(kv_heads,),
            in_specs=[
                column(count, lambda h: h, group * HD),
                column(count, lambda h: new_at + h),
                column(count, lambda h: new_at + kv_heads + h),
                column(tokens, key_at), column(tokens, value_at),
                column(tokens, key_at), column(tokens, value_at),
                column(far_rows, key_at), column(far_rows, value_at),
                column(far_rows, key_at), column(far_rows, value_at),
                pl.BlockSpec((count, HD), lambda h, place: (0, 0)),
            ],
            out_specs=column(count, lambda h: h, group * HD),
            scratch_shapes=[
                pltpu.VMEM((group * count, HD), jnp.float32),
                pltpu.VMEM((group * count, 2 * HD), jnp.float32),
            ],
        ),
        compiler_params=params,
        cost_estimate=pl.CostEstimate(
            flops=2 * count * LEN * HD * heads * 4, bytes_accessed=2**24, transcendentals=0
        ),
        name="decode",
    )(
        jnp.stack(bases).astype(jnp.int32), new, new, new, kv, kv, mate, mate,
        one, one, two, two, jnp.broadcast_to(my_limits[:, None], (count, HD)),
    )
    every = lax.all_gather(decode_out, ("seq", "section"), axis=0, tiled=False)

    of_far_key = column(far_rows, lambda h: h // group)
    of_far_value = column(far_rows, lambda h: kv_heads + h // group)
    prefill_out = pl.pallas_call(
        far_kernel,
        out_shape=jax.ShapeDtypeStruct((tokens, heads * HD), jnp.bfloat16),
        grid_spec=pltpu.PrefetchScalarGridSpec(
            num_scalar_prefetch=1,
            grid=(heads,),
            in_specs=[
                of_query, of_far_key, of_far_value, of_far_key, of_far_value, of_query, of_query,
            ],
            out_specs=of_query,
            scratch_shapes=state,
        ),
        compiler_params=params,
        cost_estimate=pl.CostEstimate(
            flops=4 * block_ops, bytes_accessed=2**26, transcendentals=0
        ),
        name="far",
    )(place, prefill_q, one, one, two, two, near, lse)

    every = every.reshape(-1, shards * count, heads * HD)
    chosen = jnp.repeat(all_cands, steps)[:, None]
    rows = every[0]
    for c in range(1, every.shape[0]):
        rows = jnp.where(chosen == c, every[c], rows)
    terms = jnp.dot(rows, out_weight, preferred_element_type=jnp.float32)
    decoded = lax.psum_scatter(terms, "heads", scatter_dimension=0, tiled=True)
    decoded = decoded.astype(jnp.bfloat16).reshape(-1, steps, out_weight.shape[1])
    return (prefill_out, decoded)


def solution(mesh):
    return jax.shard_map(
        functools.partial(body, dict(mesh.shape)),
        mesh=mesh,
        in_specs=(
            P(("groups", "seq", "section"), "heads"),
            P(("groups", "seq", "section"), None, "heads"),
            P("groups"),
            P(("groups", "seq"), None, "heads"),
            P(("groups", "seq"), None, None, "heads"),
            P(("groups", "seq")),
            P(("groups", "seq")),
            P("heads", ("seq", "section")),
        ),
        out_specs=(
            P(("groups", "seq", "section"), "heads"),
            P(("groups", "heads"), None, ("seq", "section")),
        ),
        check_vma=False,
    )
```

time: 922 us -> 373 us (0.40); the launches traced: 910 us -> 371 us
  matrix products: 469 us -> 8.01 us
  Pallas kernels: 0 us -> 275 us
  other arithmetic: 220 us -> 3.69 us
  local copies, waits for them, and re-layouts: 78.5 us -> 5.43 us
  waiting for transfers between devices: 88.1 us -> 45.9 us
  blocking collectives: 26.6 us -> 13 us
    dot_general x13 -> x1, matrix products: 469 us -> 8.01 us  [body(): terms = jnp.dot(rows, out_weight, preferred_element_type=jnp.float32)]
    pallas_call x0 -> x3, Pallas kernels: none -> 275 us  [the longest x1 141 us: body(): pl.pallas_call(near_kernel, out_shape=[jax.ShapeDtypeStruct((tokens, head...]
    reduce_sum x7 -> x1, other arithmetic: 183 us -> 0.63 us  [body(): limit = jnp.sum(jnp.where(jnp.arange(lengths.shape[0]) == cand, lengths, 0))]
    unnamed x22 -> x23, local copies, waits for them, and re-layouts: 50.7 us -> 3.33 us
    all_gather x3 -> x1, waiting for transfers between devices: 28.6 us -> 0.01 us  [body(): every = lax.all_gather(decode_out, ('seq', 'section'), axis=0, tiled=False)]
    and x5 -> x0, other arithmetic: 15.6 us -> none  [the longest x4 15.2 us: prefill_block(): (key_cand[None, :] == query_cand[:, None]) & (key_pos[None, :] <= query_p...]
    convert_element_type x3 -> x0, local copies, waits for them, and re-layouts: 13.2 us -> none  [the longest x1 12 us: body(): attended.transpose(2, 0, 1, 3).reshape(tok_local, -1).astype(jnp.bfloat16)]
    pmax x1 -> x0, blocking collectives: 12.6 us -> none  [body(): highest_all = lax.pmax(jnp.max(local_scores, axis=-1), 'seq')]
  transfers between devices with their start and end apart: 9 -> 6, of which waited for: 5 -> 1; matrix products, arithmetic and copies ran while one was open for 78% -> 1% of each run, Pallas kernels for 0% -> 69%
where the time goes in v1:
time: 373 us; the launch traced here: 371 us
  Pallas kernels  275 us (74%)
  waiting for transfers between devices  45.9 us (12%)
  between operations  14.8 us (4%)
  blocking collectives  13 us (3%)
  matrix products  8.01 us (2%)
  starting transfers between devices  5.82 us (2%)
  local copies, waits for them, and re-layouts  5.43 us (1%)
    pallas_call x1, Pallas kernels, body(): pl.pallas_call(near_kernel, out_shape=[jax.ShapeDtypeStruct((tokens, head...  141 us
    pallas_call x1, Pallas kernels, body(): pl.pallas_call(far_kernel, out_shape=jax.ShapeDtypeStruct((tokens, heads...  113 us
    ppermute x1, waiting for transfers between devices, body(): lax.ppermute(kv, 'seq', [(i, i // chips * chips + (i % chips + d) % chips...  45.8 us
    pallas_call x1, Pallas kernels, body(): pl.pallas_call(functools.partial(decode_kernel, group, steps), out_shape=...  20 us
    unnamed x1, blocking collectives  13 us
    dot_general x1, matrix products, body(): terms = jnp.dot(rows, out_weight, preferred_element_type=jnp.float32)  8.01 us
  transfers between devices with their start and end apart: 6, of which 1 were waited for; matrix products, arithmetic and copies ran while one was open for 1% of the time, Pallas kernels for 69%

profile of v1, /device:TPU:9, one launch (start us, length us, event | category | flops | bytes accessed | tf_op | source)
XLA Modules:
  0.0 371.2 jit_solution(7706585227933615485)
XLA Ops:
  7.2 0.0 all-gather.3.cloned.1.call-start
  7.2 2.2 copy.10
  9.5 0.0 copy-start.7
  9.5 0.1 collective-permute-start
  9.6 0.7 collective-permute-start.2
  10.3 45.8 %collective-permute-done.k_one.v_one = bf16[1024,1024]{1,0:T(8,128)(2,1)} collective-permute-done((bf16[1024,1024]{1,0:T(8,128)(2,1)S(1)}, bf16[1024,1024]{1,0:T(8,128)(2,1)}, u32[]{:S(2)}, u32[]{:S(2)}) %collective-permute-start) | collective-permute-done | bytes 2097184 | tf_op jit(solution)/shard_map/ppermute | solution.py:152
  56.2 1.5 collective-permute-start.1
  57.7 0.1 reshape.32
  57.9 3.2 collective-permute-start.3
  61.2 0.6 dynamic-slice
  62.4 0.2 dynamic-update-slice.1
  62.6 0.2 dynamic-update-slice
  62.8 13.0 %all-reduce.2 = (s32[64]{0:T(128)S(1)}, s32[64]{0:T(128)S(1)}) all-reduce(s32[64]{0:T(128)S(1)} %dynamic-update-slice.1, s32[64]{0:T(128)S(1)} %dynamic-update-slice), channel_id=1, replica_groups=mesh['groups'=2,'seq'=4,'heads'=2,'section'=2] {'seq'}, use_global_device_ids=true, to_apply=%add.1 | all-reduce | flops 128 | bytes 1024
  75.9 0.1 compare_select_fusion
  75.9 0.1 broadcast_in_dim.33
  76.0 0.1 broadcast_in_dim.34
  76.1 0.7 pad_add_fusion.1.place
  76.8 0.8 broadcast_in_dim.35.limits
  77.6 0.0 copy-done.3
  77.6 20.0 %decode.1 = bf16[64,4096]{1,0:T(8,128)(2,1)} custom-call(s32[4]{0:T(128)} %pad_add_fusion.1.place, bf16[64,5120]{1,0:T(8,128)(2,1)} %copy-done.3, bf16[64,5120]{1,0:T(8,128)(2,1)} %copy-done.3, bf16[64,5120]{1,0:T(8,128)(2,1)} %copy-done.3, bf16[1024,1024]{1,0:T(8,128)(2,1)} %bitcast.17, bf16[1024,1024]{1,0:T(8,128)(2,1)} %bitcast.18, ...), custom_call_target="tpu_custom_call" | custom-call | flops 8589934592 | bytes 16777216 | tf_op jit(solution)/shard_map/decode/pallas_call | solution.py:209
  97.6 0.0 all-gather.3.cloned.1.call-update
  97.6 0.2 reduce-scatter.2.cloned.1.call-start
  97.8 0.1 broadcast_in_dim.30
  97.9 0.1 eq.34
  98.0 0.6 fusion.3
  98.7 1.2 pad_add_fusion.place
  99.9 141.5 %near.1 = (f32[1024,4096]{1,0:T(8,128)}, f32[1024,4096]{1,0:T(8,128)}) custom-call(s32[4]{0:T(128)} %pad_add_fusion.place, bf16[1024,4096]{1,0:T(8,128)(2,1)} %q.3, bf16[1024,1024]{1,0:T(8,128)(2,1)} %bitcast.19, bf16[1024,1024]{1,0:T(8,128)(2,1)} %bitcast.20, bf16[1024,1024]{1,0:T(8,128)(2,1)} %collective-permute-done.2.k_mate.v_mate, ...), custom_call_target="tpu_custom_call" | custom-call | flops 51539607552 | bytes 67108864 | tf_op jit(solution)/shard_map/near/pallas_call | solution.py:178
  241.4 8.0 %fusion = f32[256,1024]{1,0:T(8,128)} fusion(bf16[4096,1024]{1,0:T(8,128)(2,1)} %param.15, bf16[512,4096]{1,0:T(8,128)(2,1)} %all-gather.3.cloned.1.call-done, pred[256]{0:T(512)(128)(4,1)S(1)} %eq.34), kind=kOutput, calls=%fused_computation.1 | convolution fusion | flops 2148532224 | bytes 13631744 | tf_op jit(solution)/shard_map/dot_general | solution.py:268
  249.4 0.0 reduce-scatter.2.cloned.1.call-update
  249.4 113.1 %far.1 = bf16[1024,4096]{1,0:T(8,128)(2,1)} custom-call(s32[4]{0:T(128)} %pad_add_fusion.place, bf16[1024,4096]{1,0:T(8,128)(2,1)} %q.3, bf16[1024,1024]{1,0:T(8,128)(2,1)} %collective-permute-done.k_one.v_one, bf16[1024,1024]{1,0:T(8,128)(2,1)} %collective-permute-done.k_one.v_one, bf16[1024,1024]{1,0:T(8,128)(2,1)} %collective-permute-done.1.k_two.v_two, ...), custom_call_target="tpu_custom_call" | custom-call | flops 68719476736 | bytes 67108864 | tf_op jit(solution)/shard_map/far/pallas_call | solution.py:244
  362.5 1.1 convert_element_type.3
  363.6 0.8 reshape.34
  (24 shorter events, 0.1 us)
Async XLA Ops:
  7.2 234.2 %all-gather.3.cloned.1.call-start = ((), (), s32[]{:S(2)}) async-start(), calls=%async_computation.2 | async-start | bytes 4718592 | tf_op jit(solution)/shard_map/all_gather | solution.py:240
  7.2 50.5 %copy-start.2 = (bf16[16,4,2,512]{3,2,1,0:T(2,128)(2,1)S(1)}, bf16[16,4,2,512]{3,2,1,0:T(2,128)(2,1)}, u32[]{:S(2)}) copy-start(bf16[16,4,2,512]{3,2,1,0:T(2,128)(2,1)} %param.12) | copy-start | bytes 393220
  7.2 50.5 %copy-start.1 = (bf16[16,4,4096]{2,1,0:T(4,128)(2,1)S(1)}, bf16[16,4,4096]{2,1,0:T(4,128)(2,1)}, u32[]{:S(2)}) copy-start(bf16[16,4,4096]{2,1,0:T(4,128)(2,1)} %param.11) | copy-start | bytes 1572868
  9.5 68.1 %copy-start = (bf16[128,8,2,512]{3,1,2,0:T(8,128)(2,1)}, bf16[128,8,2,512]{3,1,2,0:T(8,128)(2,1)S(1)}, u32[]{:S(2)}) copy-start(bf16[128,8,2,512]{3,1,2,0:T(8,128)(2,1)S(1)} %copy.10) | copy-start | bytes 6291460
  9.5 51.7 %copy-start.7 = (u32[32]{0:T(128)S(1)}, u32[32]{0:T(128)}, u32[]{:S(2)}) copy-start(u32[32]{0:T(128)} %constant.49) | copy-start | bytes 388
  9.5 52.9 %copy-start.4 = (s32[16]{0:T(128)S(1)}, s32[16]{0:T(128)}, u32[]{:S(2)}) copy-start(s32[16]{0:T(128)} %param.14) | copy-start | bytes 196
  9.5 53.1 %copy-start.5 = (s32[16]{0:T(128)S(1)}, s32[16]{0:T(128)}, u32[]{:S(2)}) copy-start(s32[16]{0:T(128)} %param.13) | copy-start | bytes 196
  9.5 46.7 %collective-permute-start = (bf16[1024,1024]{1,0:T(8,128)(2,1)S(1)}, bf16[1024,1024]{1,0:T(8,128)(2,1)}, u32[]{:S(2)}, u32[]{:S(2)}) collective-permute-start(bf16[1024,1024]{1,0:T(8,128)(2,1)S(1)} %bitcast.15), channel_id=1, source_target_pairs={{0,4},{4,0},{8,12},{12,8},{1,5},{5,1},{9,13},{13,9},{2,6},{6,2},{1... | collective-permute-start | bytes 6291464 | tf_op jit(solution)/shard_map/ppermute | solution.py:152
  9.6 67.2 %collective-permute-start.2 = (bf16[1024,1024]{1,0:T(8,128)(2,1)S(1)}, bf16[1024,1024]{1,0:T(8,128)(2,1)}, u32[]{:S(2)}, u32[]{:S(2)}) collective-permute-start(bf16[1024,1024]{1,0:T(8,128)(2,1)S(1)} %bitcast.16), channel_id=1, source_target_pairs={{0,1},{1,0},{2,3},{3,2},{4,5},{5,4},{6,7},{7,6},{8,9},{9,8},{10,11... | collective-permute-start | bytes 6291464 | tf_op jit(solution)/shard_map/ppermute | solution.py:150
  56.2 20.6 %collective-permute-start.1 = (bf16[1024,1024]{1,0:T(8,128)(2,1)}, bf16[1024,1024]{1,0:T(8,128)(2,1)}, u32[]{:S(2)}, u32[]{:S(2)}) collective-permute-start(bf16[1024,1024]{1,0:T(8,128)(2,1)} %collective-permute-done.k_one.v_one), channel_id=1, source_target_pairs={{0,1},{1,0},{2,3},{3,2},{4,5},{5,4},{6,7},{7,6},{8,9},{9,8},{10,11... | collective-permute-start | bytes 6291464 | tf_op jit(solution)/shard_map/ppermute | solution.py:196
  57.9 18.8 %collective-permute-start.3 = (bf16[64,5120]{1,0:T(8,128)(2,1)S(1)}, bf16[64,5120]{1,0:T(8,128)(2,1)S(1)}, u32[]{:S(2)}, u32[]{:S(2)}) collective-permute-start(bf16[64,5120]{1,0:T(8,128)(2,1)S(1)} %pad_maximum_fusion), channel_id=1, source_target_pairs={{0,0},{1,8},{4,1},{5,9},{8,4},{9,12},{12,5},{13,13},{2,2},{3,10},{... | collective-permute-start | bytes 1966088 | tf_op jit(solution)/shard_map/ppermute | solution.py:163
  76.8 0.8 copy-start.3
  77.6 20.4 %copy-start.6 = (s32[2]{0:T(128)S(1)}, s32[2]{0:T(128)}, u32[]{:S(2)}) copy-start(s32[2]{0:T(128)} %param.10) | copy-start | bytes 28
  97.6 264.9 %reduce-scatter.2.cloned.1.call-start = ((), (), s32[]{:S(2)}) async-start(), calls=%async_computation.1 | async-start | bytes 1572864 | tf_op jit(solution)/shard_map/reduce_scatter | solution.py:269
Sparse Core Ops, SparseCore 0:
  97.7 47.1 all-gather.2
  249.5 21.4 reduce-scatter.1

commit v2 on v1

--- a/solution.py
+++ b/solution.py
@@ -41,32 +41,48 @@
     sums_ref[...] = jnp.zeros(sums_ref.shape, jnp.float32)
 
 
-def near_kernel(place, q, k_own, v_own, k_mate, v_mate, out, lse, highest, sums):
+def near_kernel(place, q, k_own, v_own, k_mate, v_mate, out, lse):
     tokens = q.shape[0]
     tile = min(TQ, tokens)
-    start(highest, sums)
+
+    def attend(with_mate):
+        for at in range(0, tokens, tile):
+            rows = pl.ds(at, tile)
+            queries = q[rows, :]
+            last = scores_of(queries, k_own[rows, :])
+            seen = lax.broadcasted_iota(jnp.int32, last.shape, 1) <= lax.broadcasted_iota(
+                jnp.int32, last.shape, 0
+            )
+            blocks = [(jnp.where(seen, last, masked_score), v_own[rows, :])]
+            if at > 0:
+                blocks.append((scores_of(queries, k_own[:at, :]), v_own[:at, :]))
+            if with_mate:
+                blocks.append((scores_of(queries, k_mate[...]), v_mate[...]))
+            tops = [jnp.max(scores, axis=1, keepdims=True) for scores, _ in blocks]
+            top = functools.reduce(jnp.maximum, tops)
+            sums = sum(
+                jnp.dot(
+                    jnp.exp2((scores - top) * SCALE2).astype(jnp.bfloat16),
+                    with_ones(values),
+                    preferred_element_type=jnp.float32,
+                )
+                for scores, values in blocks
+            )
+            total = sums[:, HD:]
+            out[rows, :] = sums[:, :HD] / total
+            lse[rows, :] = top + jnp.log2(total) * (1.0 / SCALE2)
 
     @pl.when(place[0] == 1)
     def _():
-        for at in range(0, tokens, tile):
-            absorb(
-                highest, sums, pl.ds(at, tile), scores_of(q[pl.ds(at, tile), :], k_mate[...]), v_mate[...]
-            )
-
-    for at in range(0, tokens, tile):
-        rows = pl.ds(at, tile)
-        scores = scores_of(q[rows, :], k_own[: at + tile, :])
-        shape = scores.shape
-        seen = lax.broadcasted_iota(jnp.int32, shape, 1) <= at + lax.broadcasted_iota(
-            jnp.int32, shape, 0
-        )
-        absorb(highest, sums, rows, jnp.where(seen, scores, masked_score), v_own[: at + tile, :])
-        total = sums[rows, HD:]
-        out[rows, :] = sums[rows, :HD] / total
-        lse[rows, :] = highest[rows, :] + jnp.log2(total) * (1.0 / SCALE2)
-
-
-def far_kernel(place, q, k_one, v_one, k_two, v_two, near, lse, out, highest, sums):
+        attend(True)
+
+    @pl.when(place[0] != 1)
+    def _():
+        attend(False)
+
+
+def far_kernel(place, q, k_one, v_one, k_two, v_two, near, lse, *rest):
+    out, highest, sums = rest[-3:]
     tokens = q.shape[0]
     tile = min(TQ, tokens)
     chips, limit = place[1], place[2]
@@ -95,23 +111,22 @@
     count = q.shape[0]
     queries = jnp.concatenate([q[:, h * HD : (h + 1) * HD] for h in range(group)], axis=0)
     start(highest, sums)
-    every = pl.ds(0, group * count)
-    shape = (group * count, count)
+    half = 2 * count
+    shape = (half, count)
     asked = lax.rem(lax.broadcasted_iota(jnp.int32, shape, 0), count)
     key = lax.broadcasted_iota(jnp.int32, shape, 1)
     seen = (lax.div(asked, steps) == lax.div(key, steps)) & (key <= asked)
-    absorb(
-        highest, sums, every,
-        jnp.where(seen, scores_of(queries, k_new[...]), masked_score), v_new[...],
-    )
-    limit = jnp.concatenate([limits[:, :1]] * group, axis=0)
+    limit = jnp.concatenate([limits[:, :1]] * 2, axis=0)
+    for at in range(0, group * count, half):
+        scores = scores_of(queries[at : at + half], k_new[...])
+        absorb(highest, sums, pl.ds(at, half), jnp.where(seen, scores, masked_score), v_new[...])
 
     def block(k, v, keys, base):
-        scores = scores_of(queries, k[keys, :])
-        position = base + lax.broadcasted_iota(jnp.int32, scores.shape, 1)
-        absorb(
-            highest, sums, every, jnp.where(position < limit, scores, masked_score), v[keys, :]
-        )
+        for at in range(0, group * count, half):
+            scores = scores_of(queries[at : at + half], k[keys, :])
+            position = base + lax.broadcasted_iota(jnp.int32, scores.shape, 1)
+            scores = jnp.where(position < limit, scores, masked_score)
+            absorb(highest, sums, pl.ds(at, half), scores, v[keys, :])
 
     block(k_own, v_own, pl.ds(0, tokens), place[0])
     block(k_mate, v_mate, pl.ds(0, tokens), place[1])
@@ -183,7 +198,6 @@
             grid=(heads,),
             in_specs=[of_query, of_key, of_value, of_key, of_value],
             out_specs=[of_query, of_query],
-            scratch_shapes=state,
         ),
         compiler_params=params,
         cost_estimate=pl.CostEstimate(
@@ -192,6 +206,9 @@
         name="near",
     )(place, prefill_q, kv, kv, mate, mate)
 
+    near, lse, new, ones, all_cands, all_limits = lax.optimization_barrier(
+        (near, lse, new, ones, all_cands, all_limits)
+    )
     one = jnp.concatenate(ones, axis=0) if len(ones) > 1 else ones[0]
     two = lax.ppermute(one, "section", swap)
 
@@ -239,33 +256,43 @@
     )
     every = lax.all_gather(decode_out, ("seq", "section"), axis=0, tiled=False)
 
-    of_far_key = column(far_rows, lambda h: h // group)
-    of_far_value = column(far_rows, lambda h: kv_heads + h // group)
-    prefill_out = pl.pallas_call(
-        far_kernel,
-        out_shape=jax.ShapeDtypeStruct((tokens, heads * HD), jnp.bfloat16),
-        grid_spec=pltpu.PrefetchScalarGridSpec(
-            num_scalar_prefetch=1,
-            grid=(heads,),
-            in_specs=[
-                of_query, of_far_key, of_far_value, of_far_key, of_far_value, of_query, of_query,
-            ],
-            out_specs=of_query,
-            scratch_shapes=state,
-        ),
-        compiler_params=params,
-        cost_estimate=pl.CostEstimate(
-            flops=4 * block_ops, bytes_accessed=2**26, transcendentals=0
-        ),
-        name="far",
-    )(place, prefill_q, one, one, two, two, near, lse)
-
+    def far(place, first, number, earlier):
+        head = lambda h: first + h
+        of_query = column(tokens, head)
+        of_far_key = column(far_rows, lambda h: head(h) // group)
+        of_far_value = column(far_rows, lambda h: kv_heads + head(h) // group)
+        return pl.pallas_call(
+            far_kernel,
+            out_shape=jax.ShapeDtypeStruct((tokens, heads * HD), jnp.bfloat16),
+            grid_spec=pltpu.PrefetchScalarGridSpec(
+                num_scalar_prefetch=1,
+                grid=(number,),
+                in_specs=[
+                    of_query, of_far_key, of_far_value, of_far_key, of_far_value, of_query, of_query,
+                ]
+                + [pl.BlockSpec(memory_space=pl.ANY)] * len(earlier),
+                out_specs=of_query,
+                scratch_shapes=state,
+            ),
+            input_output_aliases={8: 0} if earlier else {},
+            compiler_params=params,
+            cost_estimate=pl.CostEstimate(
+                flops=4 * block_ops * number // heads, bytes_accessed=2**25, transcendentals=0
+            ),
+            name="far",
+        )(place, prefill_q, one, one, two, two, near, lse, *earlier)
+
+    first = heads // 2
+    prefill_out = far(place, 0, first, [])
+    every, prefill_out = lax.optimization_barrier((every, prefill_out))
     every = every.reshape(-1, shards * count, heads * HD)
     chosen = jnp.repeat(all_cands, steps)[:, None]
     rows = every[0]
     for c in range(1, every.shape[0]):
         rows = jnp.where(chosen == c, every[c], rows)
     terms = jnp.dot(rows, out_weight, preferred_element_type=jnp.float32)
+    terms, place = lax.optimization_barrier((terms, place))
+    prefill_out = far(place, first, heads - first, [prefill_out])
     decoded = lax.psum_scatter(terms, "heads", scatter_dimension=0, tiled=True)
     decoded = decoded.astype(jnp.bfloat16).reshape(-1, steps, out_weight.shape[1])
     return (prefill_out, decoded)

time: 373 us -> 338 us (0.906)
  waiting for transfers between devices: 45.9 us -> 3.5 us
  blocking collectives: 13 us -> 51.5 us
  Pallas kernels: 275 us -> 242 us
    ppermute x1, waiting for transfers between devices: 45.8 us -> 0.01 us  [body(): lax.ppermute(kv, 'seq', [(i, i // chips * chips + (i % chips + d) % chips...]
    unnamed x1, blocking collectives: 13 us -> 51.5 us
    pallas_call x1, Pallas kernels: 141 us -> 106 us  [body(): pl.pallas_call(near_kernel, out_shape=[jax.ShapeDtypeStruct((tokens, head...]
    pallas_call x1 -> x2, Pallas kernels: 113 us -> 116 us  [far(): pl.pallas_call(far_kernel, out_shape=jax.ShapeDtypeStruct((tokens, heads...]
  transfers between devices with their start and end apart: 6 -> 6, of which waited for: 1 -> 1; matrix products, arithmetic and copies ran while one was open for 1% -> 1% of each run, Pallas kernels for 69% -> 66%
where the time goes in v2:
time: 338 us; the launch traced here: 337 us
  Pallas kernels  242 us (72%)
  blocking collectives  51.5 us (15%)
  between operations  15 us (4%)
  local copies, waits for them, and re-layouts  8.73 us (3%)
  matrix products  6.71 us (2%)
  starting transfers between devices  5.59 us (2%)
  other arithmetic  4.3 us (1%)
  waiting for transfers between devices  3.5 us (1%)
    pallas_call x2, Pallas kernels, far(): pl.pallas_call(far_kernel, out_shape=jax.ShapeDtypeStruct((tokens, heads...  116 us
    pallas_call x1, Pallas kernels, body(): pl.pallas_call(near_kernel, out_shape=[jax.ShapeDtypeStruct((tokens, head...  106 us
    unnamed x1, blocking collectives  51.5 us
    pallas_call x1, Pallas kernels, body(): pl.pallas_call(functools.partial(decode_kernel, group, steps), out_shape=...  19.9 us
  transfers between devices with their start and end apart: 6, of which 1 were waited for; matrix products, arithmetic and copies ran while one was open for 1% of the time, Pallas kernels for 66%

profile of v2, /device:TPU:9, one launch (start us, length us, event | category | flops | bytes accessed | tf_op | source)
XLA Modules:
  0.0 337.4 jit_solution(2187235667548801082)
XLA Ops:
  7.2 0.0 all-gather.3.cloned.1.call-start
  7.2 2.2 copy.11
  9.5 0.7 collective-permute-start
  10.3 0.1 reshape.32
  10.5 4.5 %collective-permute-start.1 = (bf16[64,5120]{1,0:T(8,128)(2,1)S(1)}, bf16[64,5120]{1,0:T(8,128)(2,1)S(1)}, u32[]{:S(2)}, u32[]{:S(2)}) collective-permute-start(bf16[64,5120]{1,0:T(8,128)(2,1)S(1)} %pad_maximum_fusion), channel_id=1, source_target_pairs={{0,0},{1,8},{4,1},{5,9},{8,4},{9,12},{12,5},{13,13},{2,2},{3,10},{... | collective-permute-start | bytes 1966088 | tf_op jit(solution)/shard_map/ppermute | solution.py:178
  15.0 0.7 dynamic-slice
  16.4 0.2 dynamic-update-slice
  16.7 0.2 dynamic-update-slice.1
  16.9 51.5 %all-reduce.2 = (s32[64]{0:T(128)S(1)}, s32[64]{0:T(128)S(1)}) all-reduce(s32[64]{0:T(128)S(1)} %dynamic-update-slice, s32[64]{0:T(128)S(1)} %dynamic-update-slice.1), channel_id=1, replica_groups=mesh['groups'=2,'seq'=4,'heads'=2,'section'=2] {'seq'}, use_global_device_ids=true, to_apply=%add | all-reduce | flops 128 | bytes 1024
  68.4 0.7 fusion
  69.1 1.3 pad_add_fusion.place
  70.4 106.1 %near.1 = (f32[1024,4096]{1,0:T(8,128)}, f32[1024,4096]{1,0:T(8,128)}) custom-call(s32[4]{0:T(128)} %pad_add_fusion.place, bf16[1024,4096]{1,0:T(8,128)(2,1)} %q.5, bf16[1024,1024]{1,0:T(8,128)(2,1)} %bitcast.24, bf16[1024,1024]{1,0:T(8,128)(2,1)} %bitcast.25, bf16[1024,1024]{1,0:T(8,128)(2,1)} %collective-permute-done.k_mate.v_mate, ...), custom_call_target="tpu_custom_call" | custom-call | flops 51539607552 | bytes 67108864 | tf_op jit(solution)/shard_map/near/pallas_call | solution.py:193
  176.5 0.1 collective-permute-start.3
  176.6 0.6 pad_add_fusion.1.place
  177.3 0.1 compare_select_fusion
  177.3 0.1 broadcast_in_dim.33
  177.4 0.1 broadcast_in_dim.34
  177.5 3.5 %collective-permute-done.3.k_two.v_two = bf16[1024,1024]{1,0:T(8,128)(2,1)S(1)} collective-permute-done((bf16[1024,1024]{1,0:T(8,128)(2,1)}, bf16[1024,1024]{1,0:T(8,128)(2,1)S(1)}, u32[]{:S(2)}, u32[]{:S(2)}) %collective-permute-start.3) | collective-permute-done | bytes 2097184 | tf_op jit(solution)/shard_map/ppermute | solution.py:213
  181.0 0.8 broadcast_in_dim.35.limits
  181.8 0.5 copy-done.3
  182.3 19.9 %decode.1 = bf16[64,4096]{1,0:T(8,128)(2,1)} custom-call(s32[4]{0:T(128)} %pad_add_fusion.1.place, bf16[64,5120]{1,0:T(8,128)(2,1)} %copy-done.4, bf16[64,5120]{1,0:T(8,128)(2,1)} %copy-done.4, bf16[64,5120]{1,0:T(8,128)(2,1)} %copy-done.4, bf16[1024,1024]{1,0:T(8,128)(2,1)} %bitcast.26, bf16[1024,1024]{1,0:T(8,128)(2,1)} %bitcast.27, ...), custom_call_target="tpu_custom_call" | custom-call | flops 8589934592 | bytes 16777216 | tf_op jit(solution)/shard_map/decode/pallas_call | solution.py:226
  202.2 0.2 reduce-scatter.2.cloned.1.call-start
  202.4 0.1 broadcast_in_dim.30
  202.5 0.1 eq.34
  202.6 58.0 %far.2.rest_0_ = bf16[1024,4096]{1,0:T(8,128)(2,1)} custom-call(s32[4]{0:T(128)} %pad_add_fusion.place, bf16[1024,4096]{1,0:T(8,128)(2,1)} %q.5, bf16[1024,1024]{1,0:T(8,128)(2,1)} %collective-permute-done.2.k_one.v_one, bf16[1024,1024]{1,0:T(8,128)(2,1)} %collective-permute-done.2.k_one.v_one, bf16[1024,1024]{1,0:T(8,128)(2,1)} %copy-done.3, ...), custom_call_target="tpu_custom_call" | custom-call | flops 34359738368 | bytes 33554432 | tf_op jit(solution)/shard_map/far/pallas_call | solution.py:264
  260.6 2.7 fusion.1
  263.4 0.5 bitcast_select_fusion
  263.8 6.7 %fusion.2 = f32[256,1024]{1,0:T(8,128)} fusion(bf16[256,4096]{1,0:T(8,128)(2,1)S(1)} %bitcast_select_fusion, bf16[4096,1024]{1,0:T(8,128)(2,1)} %param.15), kind=kOutput, calls=%fused_computation.9 | convolution fusion | flops 2147483648 | bytes 11534336 | tf_op jit(solution)/shard_map/dot_general | solution.py:293
  270.6 0.0 reduce-scatter.2.cloned.1.call-update
  270.6 58.1 %far.3 = bf16[1024,4096]{1,0:T(8,128)(2,1)} custom-call(s32[4]{0:T(128)} %pad_add_fusion.place, bf16[1024,4096]{1,0:T(8,128)(2,1)} %q.5, bf16[1024,1024]{1,0:T(8,128)(2,1)} %collective-permute-done.2.k_one.v_one, bf16[1024,1024]{1,0:T(8,128)(2,1)} %collective-permute-done.2.k_one.v_one, ...), custom_call_target="tpu_custom_call", output_to_operand_aliasing={{}: (8, {})} | custom-call | flops 34359738368 | bytes 33554432 | tf_op jit(solution)/shard_map/far/pallas_call | solution.py:264
  328.7 1.1 convert_element_type.3
  329.8 0.8 reshape.34
  (29 shorter events, 0.1 us)
Async XLA Ops:
  7.2 253.5 %all-gather.3.cloned.1.call-start = ((), (), s32[]{:S(2)}) async-start(), calls=%async_computation.2 | async-start | bytes 4718592 | tf_op jit(solution)/shard_map/all_gather | solution.py:257
  7.2 3.0 copy-start.2
  7.2 3.1 copy-start.1
  9.5 60.9 %copy-start = (bf16[128,8,2,512]{3,1,2,0:T(8,128)(2,1)}, bf16[128,8,2,512]{3,1,2,0:T(8,128)(2,1)S(1)}, u32[]{:S(2)}) copy-start(bf16[128,8,2,512]{3,1,2,0:T(8,128)(2,1)S(1)} %copy.11) | copy-start | bytes 6291460
  9.5 5.6 %copy-start.8 = (u32[32]{0:T(128)S(1)}, u32[32]{0:T(128)}, u32[]{:S(2)}) copy-start(u32[32]{0:T(128)} %constant.49) | copy-start | bytes 388
  9.5 6.9 %copy-start.5 = (s32[16]{0:T(128)S(1)}, s32[16]{0:T(128)}, u32[]{:S(2)}) copy-start(s32[16]{0:T(128)} %param.13) | copy-start | bytes 196
  9.5 7.2 %copy-start.6 = (s32[16]{0:T(128)S(1)}, s32[16]{0:T(128)}, u32[]{:S(2)}) copy-start(s32[16]{0:T(128)} %param.14) | copy-start | bytes 196
  9.5 58.9 %copy-start.7 = (s32[2]{0:T(128)S(1)}, s32[2]{0:T(128)}, u32[]{:S(2)}) copy-start(s32[2]{0:T(128)} %param.10) | copy-start | bytes 28
  9.5 60.8 %collective-permute-start = (bf16[1024,1024]{1,0:T(8,128)(2,1)S(1)}, bf16[1024,1024]{1,0:T(8,128)(2,1)}, u32[]{:S(2)}, u32[]{:S(2)}) collective-permute-start(bf16[1024,1024]{1,0:T(8,128)(2,1)S(1)} %bitcast.22), channel_id=1, source_target_pairs={{0,1},{1,0},{2,3},{3,2},{4,5},{5,4},{6,7},{7,6},{8,9},{9,8},{10,11... | collective-permute-start | bytes 6291464 | tf_op jit(solution)/shard_map/ppermute | solution.py:165
  10.3 166.3 %collective-permute-start.2 = (bf16[1024,1024]{1,0:T(8,128)(2,1)S(1)}, bf16[1024,1024]{1,0:T(8,128)(2,1)}, u32[]{:S(2)}, u32[]{:S(2)}) collective-permute-start(bf16[1024,1024]{1,0:T(8,128)(2,1)S(1)} %bitcast.23), channel_id=1, source_target_pairs={{0,4},{4,0},{8,12},{12,8},{1,5},{5,1},{9,13},{13,9},{2,6},{6,2},{1... | collective-permute-start | bytes 6291464 | tf_op jit(solution)/shard_map/ppermute | solution.py:167
  10.5 166.0 %collective-permute-start.1 = (bf16[64,5120]{1,0:T(8,128)(2,1)S(1)}, bf16[64,5120]{1,0:T(8,128)(2,1)S(1)}, u32[]{:S(2)}, u32[]{:S(2)}) collective-permute-start(bf16[64,5120]{1,0:T(8,128)(2,1)S(1)} %pad_maximum_fusion), channel_id=1, source_target_pairs={{0,0},{1,8},{4,1},{5,9},{8,4},{9,12},{12,5},{13,13},{2,2},{3,10},{... | collective-permute-start | bytes 1966088 | tf_op jit(solution)/shard_map/ppermute | solution.py:178
  176.5 5.3 %copy-start.4 = (bf16[64,5120]{1,0:T(8,128)(2,1)}, bf16[64,5120]{1,0:T(8,128)(2,1)S(1)}, u32[]{:S(2)}) copy-start(bf16[64,5120]{1,0:T(8,128)(2,1)S(1)} %collective-permute-done.1.q.k_new.v_new) | copy-start | bytes 1966084
  176.5 4.4 %collective-permute-start.3 = (bf16[1024,1024]{1,0:T(8,128)(2,1)}, bf16[1024,1024]{1,0:T(8,128)(2,1)S(1)}, u32[]{:S(2)}, u32[]{:S(2)}) collective-permute-start(bf16[1024,1024]{1,0:T(8,128)(2,1)} %collective-permute-done.2.k_one.v_one), channel_id=1, source_target_pairs={{0,1},{1,0},{2,3},{3,2},{4,5},{5,4},{6,7},{7,6},{8,9},{9,8},{10,11... | collective-permute-start | bytes 6291464 | tf_op jit(solution)/shard_map/ppermute | solution.py:213
  181.0 1.3 copy-start.3
  202.2 126.5 %reduce-scatter.2.cloned.1.call-start = ((), (), s32[]{:S(2)}) async-start(), calls=%async_computation.1 | async-start | bytes 1572864 | tf_op jit(solution)/shard_map/reduce_scatter | solution.py:296
Sparse Core Ops, SparseCore 0:
  202.3 44.6 all-gather.2
  270.7 18.9 reduce-scatter.1
